TPU v7x, 512 devices: a whole 4x8x8 slice. The times are simulated.
512 devices in a mesh: tile: 128 (over y, z, core), clip: 4 (over x).
Axes of the slice: x: 4, y: 8, z: 8, core: 2. Of those that a mesh axis runs over, the one named last changes fastest.
Arguments:
- features: bfloat16 [4, 128, 96, 3, 4096], P('clip', 'tile'), may hold values from -6 to 6
- conv_weight: bfloat16 [3, 9, 3, 96], replicated, may hold values from -0.125 to 0.125
- bias: float32 [3], replicated, may hold values from -2 to 2
- blend_profile: int32 [32], replicated, may hold values from 1 to 8
- tile_ids: int32 [4, 128], P('clip'), may hold values from 0 to 127, each once within a row
- reward_grad: bfloat16 [4, 128, 3, 4096], P('clip', 'tile'), may hold values from -6 to 6
Outputs:
- decoded: bfloat16 [4, 128, 3, 4096], P('clip', 'tile')
- feature_grad: bfloat16 [4, 128, 96, 3, 4096], P('clip', 'tile')
- weight_grad: float32 [3, 9, 3, 96], replicated
- bias_grad: float32 [3], replicated
Inputs may be any that keep to these rules, and one draw needn't show every extreme that they name: Each row of tile_ids names each of the 128 tiles of the window once; tile v lies in tile row v // 16 and tile column v % 16.
All inputs are finite; a program needn't handle non-finite values.
Results may differ from a plain program's by a relative error of at most 0.023.
Values may be sent and summed in bfloat16 or wider, within the bound.
No kernel may reach another device: no remote copies, remote signals or barrier semaphores. Data moves between devices by JAX's collectives and lax.ppermute only.
A program may use at most 64 MiB of HBM per device.

v0:
```python
import math
import jax
import jax.numpy as jnp
from jax import lax
from jax.sharding import PartitionSpec as P

neighbour_steps = [(-1, -1), (-1, 0), (-1, 1), (0, -1), (0, 1), (1, -1), (1, 0), (1, 1)]


def cut_region(tile_block, step_y, step_x, intersection):
    edge = tile_block.shape[-1]
    if step_y == 1:
        tile_block = tile_block[..., :intersection, :]
    elif step_y == -1:
        tile_block = tile_block[..., edge - intersection :, :]
    if step_x == 1:
        tile_block = tile_block[..., :intersection]
    elif step_x == -1:
        tile_block = tile_block[..., edge - intersection :]
    return tile_block


def place_region(region, step_y, step_x, stride):
    pad_y = (stride, 0) if step_y == 1 else (0, stride) if step_y == -1 else (0, 0)
    pad_x = (stride, 0) if step_x == 1 else (0, stride) if step_x == -1 else (0, 0)
    return jnp.pad(region, ((0, 0),) * (region.ndim - 2) + (pad_y, pad_x))


def pick_regions(gathered, neighbours, intersection, edge):
    regions = []
    for step_y, step_x, present, holder in neighbours:
        whole_tile = lax.dynamic_index_in_dim(gathered, holder, keepdims=False)
        whole_tile = whole_tile.reshape(whole_tile.shape[0], edge, edge)
        regions.append(cut_region(whole_tile, step_y, step_x, intersection))
    return regions


def per_device(features, conv_weight, bias, blend_profile, tile_ids, reward_grad):
    pixels = features.shape[-1]
    edge = math.isqrt(pixels)
    intersection = blend_profile.shape[0]
    stride = edge - intersection
    colours = conv_weight.shape[2]
    channels = conv_weight.shape[3]
    slots = tile_ids.shape[1]
    own_index = lax.axis_index("tile")
    peer_count = lax.axis_size("tile")
    tiles_across = min(16, peer_count)
    tile_count_rows = slots // tiles_across
    tile_list = tile_ids[0]
    mine = lax.dynamic_index_in_dim(tile_list, own_index, keepdims=False)
    my_row = mine // tiles_across
    my_col = mine % tiles_across
    places = jnp.arange(slots, dtype=jnp.int32)
    neighbours = []
    for step_y, step_x in neighbour_steps:
        tile_row = my_row + step_y
        tile_col = my_col + step_x
        present = (
            (tile_row >= 0)
            & (tile_row < tile_count_rows)
            & (tile_col >= 0)
            & (tile_col < tiles_across)
        )
        target = tile_row * tiles_across + tile_col
        holder = jnp.sum(jnp.where(tile_list == target, places, 0))
        neighbours.append((step_y, step_x, present, holder))
    distance_range = jnp.arange(edge)
    distance = jnp.minimum(jnp.minimum(distance_range, edge - 1 - distance_range), intersection - 1)
    lookup = (distance[:, None] == jnp.arange(intersection)[None, :]).astype(jnp.float32)
    factor = jnp.dot(lookup, blend_profile.astype(jnp.float32))
    weight_map = factor[:, None] * factor[None, :]
    frames = features[0, 0]
    kernel = conv_weight.reshape(conv_weight.shape[0], 9 * colours, channels)
    tap_sums = jnp.einsum("tjc,ctp->jp", kernel, frames, preferred_element_type=jnp.float32)
    tap_sums = tap_sums.reshape(3, 3, colours, edge, edge)
    padded = jnp.pad(tap_sums, ((0, 0), (0, 0), (0, 0), (1, 1), (1, 1)))
    tile_image = jnp.broadcast_to(bias[:, None, None], (colours, edge, edge))
    for shift_y in range(3):
        for shift_x in range(3):
            tile_image = (
                tile_image
                + padded[shift_y, shift_x, :, shift_y : shift_y + edge, shift_x : shift_x + edge]
            )
    tile_image = tile_image.astype(jnp.bfloat16)
    cotangent = reward_grad[0, 0]
    gathered_images = lax.all_gather(
        tile_image.reshape(1, colours, pixels), "tile", axis=0, tiled=True
    )
    gathered_grads = lax.all_gather(
        cotangent.reshape(1, colours, pixels), "tile", axis=0, tiled=True
    )
    forward_regions = pick_regions(gathered_images, neighbours, intersection, edge)
    backward_regions = pick_regions(gathered_grads, neighbours, intersection, edge)
    numerator = weight_map * tile_image.astype(jnp.float32)
    weight_total = weight_map
    summed = cotangent.astype(jnp.float32).reshape(colours, edge, edge)
    for (step_y, step_x, present, holder), image_part, grad_part in zip(
        neighbours, forward_regions, backward_regions
    ):
        present_mask = present.astype(jnp.float32)
        part_weight = place_region(
            cut_region(weight_map, step_y, step_x, intersection), step_y, step_x, stride
        )
        numerator = numerator + present_mask * part_weight * place_region(
            image_part.astype(jnp.float32), step_y, step_x, stride
        )
        weight_total = weight_total + present_mask * part_weight
        summed = summed + present_mask * place_region(
            grad_part.astype(jnp.float32), step_y, step_x, stride
        )
    decoded = (numerator / weight_total).astype(jnp.bfloat16).reshape(1, 1, colours, pixels)
    image_grad = (weight_map / weight_total * summed).astype(jnp.bfloat16)
    grad_padded = jnp.pad(image_grad, ((0, 0), (1, 1), (1, 1)))
    shifted = []
    for shift_y in range(3):
        for shift_x in range(3):
            shifted.append(
                grad_padded[:, 2 - shift_y : 2 - shift_y + edge, 2 - shift_x : 2 - shift_x + edge]
            )
    grad_stack = jnp.stack(shifted, 0).reshape(9 * colours, pixels)
    value_grad = jnp.einsum("tjc,jp->ctp", kernel, grad_stack, preferred_element_type=jnp.float32)
    feature_grad = value_grad.astype(jnp.bfloat16).reshape(1, 1, channels, frames.shape[1], pixels)
    kernel_local = jnp.einsum("jp,ctp->tjc", grad_stack, frames, preferred_element_type=jnp.float32)
    bias_local = jnp.sum(image_grad.astype(jnp.float32), axis=(1, 2))
    kernel_total, bias_total = lax.psum((kernel_local, bias_local), ("tile", "clip"))
    grad_scale = 1.0 / math.sqrt(lax.axis_size("clip") * lax.axis_size("tile") * pixels)
    weight_grad = (kernel_total * grad_scale).reshape(conv_weight.shape[0], 9, colours, channels)
    bias_grad = bias_total * grad_scale
    return (decoded, feature_grad, weight_grad, bias_grad)


def solution(mesh):
    return jax.shard_map(
        per_device,
        mesh=mesh,
        in_specs=(
            P("clip", "tile", None, None, None),
            P(),
            P(),
            P(),
            P("clip", None),
            P("clip", "tile", None, None),
        ),
        out_specs=(P("clip", "tile", None, None), P("clip", "tile", None, None, None), P(), P()),
        check_vma=False,
    )
```

profile of v0, /device:TPU:1, one launch (start us, length us, event | category | flops | bytes accessed | tf_op | source)
XLA Modules:
  0.0 295.1 jit_solution(15663109818594018392)
XLA Ops:
  8.0 4.5 %copy.34 = bf16[1,1,96,3,4096]{2,4,3,1,0:T(8,128)(2,1)} copy(bf16[1,1,96,3,4096]{4,2,3,1,0:T(8,128)(2,1)} %param.6) | data formatting | bytes 4718592 | tf_op args[0]
  13.1 4.0 %fusion.5 = f32[3,3,3,64,64]{4,2,3,1,0:T(4,128)S(1)} fusion(bf16[64,64,96,3,1,1]{2,1,0,3,5,4:T(8,128)(2,1)} %bitcast.182, bf16[3,3,3,96,3]{3,2,1,0,4:T(4,128)(2,1)S(1)} %dot_general.22), kind=kOutput, calls=%fused_computation.6 | convolution fusion | flops 63700992 | bytes 2817216 | tf_op jit(solution)/shard_map/tjc,ctp->jp/dot_general | solution.py:75
  23.1 0.8 fusion.16
  33.8 0.7 reshape.284
  41.4 0.7 multiply_divide_fusion
  42.1 59.6 %all-gather.6.cloned.1.call-done = bf16[128,1,3,4096]{3,2,1,0:T(4,128)(2,1)} async-done(((bf16[1,1,3,4096]{3,2,1,0:T(4,128)(2,1)}), bf16[128,1,3,4096]{3,2,1,0:T(4,128)(2,1)}) %all-gather.6.cloned.1.call-update) | async-done | bytes 3145744 | tf_op jit(solution)/shard_map/all_gather | solution.py:90
  101.8 1.0 constant_dynamic-slice_fusion.7
  104.9 0.7 reshape.277
  105.8 0.7 slice.210
  107.9 0.7 reshape.273
  108.6 1.0 slice.207
  109.6 1.3 convert_reduce_fusion
  110.8 0.7 bitcast_dynamic-update-slice_fusion.8
  112.2 0.7 bitcast_dynamic-update-slice_fusion.6
  114.9 0.7 bitcast_dynamic-update-slice_fusion.2
  116.3 0.7 bitcast_dynamic-update-slice_fusion
  117.0 2.1 reshape.307
  119.1 3.2 %fusion = bf16[1,1,96,3,4096]{4,2,3,1,0:T(8,128)(2,1)} fusion(bf16[27,4096,1]{1,0,2:T(8,128)(2,1)} %reshape.307, bf16[3,27,96]{2,1,0:T(8,128)(2,1)} %copy-done.3), kind=kOutput, calls=%fused_computation.1 | convolution fusion | flops 64880640 | bytes 2596032 | tf_op jit(solution)/shard_map/tjc,jp->ctp/dot_general | solution.py:122
  122.3 1.5 fusion.8
  123.8 62.6 %all-gather.4.cloned.1.call-done = bf16[128,3,4096]{2,1,0:T(4,128)(2,1)} async-done(((bf16[1,3,4096]{2,1,0:T(4,128)(2,1)}), bf16[128,3,4096]{2,1,0:T(4,128)(2,1)}) %all-gather.4.cloned.1.call-update) | async-done | bytes 3145744 | tf_op jit(solution)/shard_map/all_gather | solution.py:87
  186.4 1.0 constant_dynamic-slice_fusion.15
  188.7 1.5 fusion.12
  190.3 0.7 reshape.272
  191.0 96.1 %all-reduce.26 = (f32[3,27,96]{2,1,0:T(8,128)S(1)}, f32[3]{0:T(128)S(1)}) all-reduce(f32[3,27,96]{2,1,0:T(8,128)S(1)} %copy-done.4, f32[3]{0:T(128)S(1)} %get-tuple-element.14), channel_id=1, replica_groups=mesh['tile'=128,'clip'=4] {'tile','clip'}, use_global_device_ids=true, to_apply=%region_8.9 | all-reduce | flops 7779 | bytes 62232 | tf_op jit(solution)/shard_map/psum | solution.py:126
  (99 shorter events, 15.7 us)
Async XLA Ops:
  7.2 94.6 %all-gather.6.cloned.1.call-start = ((), (), s32[]{:S(2)}) async-start(), calls=%async_computation.1 | async-start | bytes 4227072 | tf_op jit(solution)/shard_map/all_gather | solution.py:90
  7.9 4.6 %copy-start.6 = (bf16[3,9,3,96]{3,2,1,0:T(4,128)(2,1)S(1)}, bf16[3,9,3,96]{3,2,1,0:T(4,128)(2,1)}, u32[]{:S(2)}) copy-start(bf16[3,9,3,96]{3,2,1,0:T(4,128)(2,1)} %param.7) | copy-start | bytes 46660
  7.9 178.5 %all-gather.4.cloned.1.call-start = ((), (), s32[]{:S(2)}) async-start(), calls=%async_computation | async-start | bytes 4227072 | tf_op jit(solution)/shard_map/all_gather | solution.py:87
  12.5 0.6 copy-start.3
  17.1 1.7 copy-start.7
  17.6 2.2 copy-start.8
  17.7 16.2 %copy-start.5 = (bf16[1,1,3,4096]{3,2,1,0:T(4,128)(2,1)S(1)}, bf16[1,1,3,4096]{3,2,1,0:T(4,128)(2,1)}, u32[]{:S(2)}) copy-start(bf16[1,1,3,4096]{3,2,1,0:T(4,128)(2,1)} %param.11) | copy-start | bytes 73732
  17.7 21.9 %copy-start.9 = (s32[32]{0:T(128)S(1)}, s32[32]{0:T(128)}, u32[]{:S(2)}) copy-start(s32[32]{0:T(128)} %param.9) | copy-start | bytes 388
  39.9 1.4 copy-start.2
  108.6 13.7 %copy-start = (bf16[1,1,96,3,4096]{4,2,3,1,0:T(8,128)(2,1)S(1)}, bf16[1,1,96,3,4096]{4,2,3,1,0:T(8,128)(2,1)}, u32[]{:S(2)}) copy-start(bf16[1,1,96,3,4096]{4,2,3,1,0:T(8,128)(2,1)} %param.6) | copy-start | bytes 7077892
  119.1 3.3 %copy-start.1 = (bf16[27,4096,1]{1,0,2:T(8,128)(2,1)S(1)}, bf16[27,4096,1]{1,0,2:T(8,128)(2,1)}, u32[]{:S(2)}) copy-start(bf16[27,4096,1]{1,0,2:T(8,128)(2,1)} %reshape.307) | copy-start | bytes 663556
  123.8 67.2 %copy-start.4 = (f32[3,27,96]{2,1,0:T(8,128)S(1)}, f32[3,27,96]{2,1,0:T(8,128)}, u32[]{:S(2)}) copy-start(f32[3,27,96]{2,1,0:T(8,128)} %fusion.8) | copy-start | bytes 93316
Sparse Core Ops, SparseCore 0:
  11.1 90.5 all-gather.5
  104.9 81.4 all-gather.3
where the time goes:
time: 296 us; the launch traced here: 295 us
  waiting for transfers between devices  123 us (42%)
  blocking collectives  96.1 us (32%)
  between operations  32 us (11%)
  local copies, waits for them, and re-layouts  28.5 us (10%)
  matrix products  8.93 us (3%)
  other arithmetic  6.52 us (2%)
    psum x1, blocking collectives, per_device(): lax.psum((kernel_local, bias_local), ('tile', 'clip'))  96.1 us
    all_gather x1, waiting for transfers between devices, per_device(): lax.all_gather(tile_image.reshape(1, colours, pixels), 'tile', axis=0, ti...  62.6 us
    all_gather x1, waiting for transfers between devices, per_device(): lax.all_gather(cotangent.reshape(1, colours, pixels), 'tile', axis=0, til...  59.6 us
    unnamed x37, local copies, waits for them, and re-layouts  10.8 us
  transfers between devices with their start and end apart: 2, of which 2 were waited for; matrix products, arithmetic and copies ran while one was open for 13% of the time, Pallas kernels for 0%

commit v1 on v0

--- a/solution.py
+++ b/solution.py
@@ -123,7 +123,7 @@
     feature_grad = value_grad.astype(jnp.bfloat16).reshape(1, 1, channels, frames.shape[1], pixels)
     kernel_local = jnp.einsum("jp,ctp->tjc", grad_stack, frames, preferred_element_type=jnp.float32)
     bias_local = jnp.sum(image_grad.astype(jnp.float32), axis=(1, 2))
-    kernel_total, bias_total = lax.psum((kernel_local, bias_local), ("tile", "clip"))
+    kernel_total, bias_total = lax.psum(lax.psum((kernel_local, bias_local), "tile"), "clip")
     grad_scale = 1.0 / math.sqrt(lax.axis_size("clip") * lax.axis_size("tile") * pixels)
     weight_grad = (kernel_total * grad_scale).reshape(conv_weight.shape[0], 9, colours, channels)
     bias_grad = bias_total * grad_scale

time: 296 us -> 708 us (2.39)
  blocking collectives: 96.1 us -> 502 us
    psum x1 -> x2, blocking collectives: 96.1 us -> 502 us  [the longest x1 488 us: per_device(): lax.psum((kernel_local, bias_local), 'tile')]
  transfers between devices with their start and end apart: 2 -> 2, of which waited for: 2 -> 2; matrix products, arithmetic and copies ran while one was open for 13% -> 5% of each run, Pallas kernels for 0% -> 0%
where the time goes in v1:
time: 708 us; the launch traced here: 701 us
  blocking collectives  502 us (71%)
  waiting for transfers between devices  123 us (17%)
  between operations  32 us (5%)
  local copies, waits for them, and re-layouts  28.5 us (4%)
  matrix products  8.93 us (1%)
    psum x1, blocking collectives, per_device(): lax.psum((kernel_local, bias_local), 'tile')  488 us
    all_gather x1, waiting for transfers between devices, per_device(): lax.all_gather(tile_image.reshape(1, colours, pixels), 'tile', axis=0, ti...  62.6 us
    all_gather x1, waiting for transfers between devices, per_device(): lax.all_gather(cotangent.reshape(1, colours, pixels), 'tile', axis=0, til...  59.6 us
  transfers between devices with their start and end apart: 2, of which 2 were waited for; matrix products, arithmetic and copies ran while one was open for 5% of the time, Pallas kernels for 0%

profile of v1, /device:TPU:1, one launch (start us, length us, event | category | flops | bytes accessed | tf_op | source)
XLA Modules:
  0.0 700.8 jit_solution(16817103576407163071)
XLA Ops:
  8.0 4.5 copy.34
  13.1 4.0 fusion.5
  23.1 0.8 fusion.16
  33.8 0.7 reshape.284
  41.4 0.7 multiply_divide_fusion
  42.1 59.6 %all-gather.6.cloned.1.call-done = bf16[128,1,3,4096]{3,2,1,0:T(4,128)(2,1)} async-done(((bf16[1,1,3,4096]{3,2,1,0:T(4,128)(2,1)}), bf16[128,1,3,4096]{3,2,1,0:T(4,128)(2,1)}) %all-gather.6.cloned.1.call-update) | async-done | bytes 3145744 | tf_op jit(solution)/shard_map/all_gather | solution.py:90
  101.8 1.0 constant_dynamic-slice_fusion.7
  104.9 0.7 reshape.277
  105.8 0.7 slice.210
  107.9 0.7 reshape.273
  108.6 1.0 slice.207
  109.6 1.3 convert_reduce_fusion
  110.8 0.7 bitcast_dynamic-update-slice_fusion.8
  112.2 0.7 bitcast_dynamic-update-slice_fusion.6
  114.9 0.7 bitcast_dynamic-update-slice_fusion.2
  117.0 2.1 reshape.307
  119.1 3.2 fusion
  122.3 1.5 fusion.8
  123.8 62.6 %all-gather.4.cloned.1.call-done = bf16[128,3,4096]{2,1,0:T(4,128)(2,1)} async-done(((bf16[1,3,4096]{2,1,0:T(4,128)(2,1)}), bf16[128,3,4096]{2,1,0:T(4,128)(2,1)}) %all-gather.4.cloned.1.call-update) | async-done | bytes 3145744 | tf_op jit(solution)/shard_map/all_gather | solution.py:87
  186.4 1.0 constant_dynamic-slice_fusion.15
  188.7 1.5 fusion.12
  190.3 0.7 reshape.272
  191.0 488.0 %all-reduce.26 = (f32[3,27,96]{2,1,0:T(8,128)S(1)}, f32[3]{0:T(128)S(1)}) all-reduce(f32[3,27,96]{2,1,0:T(8,128)S(1)} %copy-done.4, f32[3]{0:T(128)S(1)} %get-tuple-element.16), channel_id=1, replica_groups=mesh['tile'=128,'clip'=4] {'tile'}, use_global_device_ids=true, to_apply=%region_8.9 | all-reduce | flops 7779 | bytes 62232 | tf_op jit(solution)/shard_map/psum | solution.py:126
  679.0 13.7 %all-reduce.27 = (f32[3,27,96]{2,1,0:T(8,128)S(1)}, f32[3]{0:T(128)S(1)}) all-reduce(f32[3,27,96]{2,1,0:T(8,128)S(1)} %get-tuple-element.12, f32[3]{0:T(128)S(1)} %get-tuple-element.13), channel_id=1, replica_groups=mesh['tile'=128,'clip'=4] {'clip'}, use_global_device_ids=true, to_apply=%region_9.10 | all-reduce | flops 7779 | bytes 62232 | tf_op jit(solution)/shard_map/psum | solution.py:126
  (100 shorter events, 16.5 us)
Async XLA Ops:
  7.2 94.6 %all-gather.6.cloned.1.call-start = ((), (), s32[]{:S(2)}) async-start(), calls=%async_computation.1 | async-start | bytes 4227072 | tf_op jit(solution)/shard_map/all_gather | solution.py:90
  7.9 4.6 copy-start.6
  7.9 178.5 %all-gather.4.cloned.1.call-start = ((), (), s32[]{:S(2)}) async-start(), calls=%async_computation | async-start | bytes 4227072 | tf_op jit(solution)/shard_map/all_gather | solution.py:87
  12.5 0.6 copy-start.3
  17.1 1.7 copy-start.7
  17.6 2.2 copy-start.8
  17.7 16.2 %copy-start.5 = (bf16[1,1,3,4096]{3,2,1,0:T(4,128)(2,1)S(1)}, bf16[1,1,3,4096]{3,2,1,0:T(4,128)(2,1)}, u32[]{:S(2)}) copy-start(bf16[1,1,3,4096]{3,2,1,0:T(4,128)(2,1)} %param.11) | copy-start | bytes 73732
  17.7 21.9 %copy-start.9 = (s32[32]{0:T(128)S(1)}, s32[32]{0:T(128)}, u32[]{:S(2)}) copy-start(s32[32]{0:T(128)} %param.9) | copy-start | bytes 388
  39.9 1.4 copy-start.2
  108.6 13.7 %copy-start = (bf16[1,1,96,3,4096]{4,2,3,1,0:T(8,128)(2,1)S(1)}, bf16[1,1,96,3,4096]{4,2,3,1,0:T(8,128)(2,1)}, u32[]{:S(2)}) copy-start(bf16[1,1,96,3,4096]{4,2,3,1,0:T(8,128)(2,1)} %param.6) | copy-start | bytes 7077892
  119.1 3.3 copy-start.1
  123.8 67.2 %copy-start.4 = (f32[3,27,96]{2,1,0:T(8,128)S(1)}, f32[3,27,96]{2,1,0:T(8,128)}, u32[]{:S(2)}) copy-start(f32[3,27,96]{2,1,0:T(8,128)} %fusion.8) | copy-start | bytes 93316
Sparse Core Ops, SparseCore 0:
  11.1 90.5 all-gather.5
  104.9 81.4 all-gather.3
